TPU v7x, 256 devices: a whole 4x4x8 slice. The times are simulated.
256 devices in a mesh: grp: 16 (over y_lo, x, core), tok: 16 (over z, y_hi).
Axes of the slice: x: 4, y: 4 (y_hi: 2, y_lo: 2; y = y_hi * 2 + y_lo), z: 8, core: 2. Of those that a mesh axis runs over, the one named last changes fastest.
Arguments:
- acts: bfloat16 [4096, 8192], P('tok', 'grp'), may hold values from -6 to 6
- grads: bfloat16 [4096, 8192], P('tok', 'grp'), may hold values from -6 to 6
- basis_in: bfloat16 [8192, 8192], P('tok', 'grp'), may hold values from -0.0625 to 0.0625
- basis_out: bfloat16 [8192, 8192], P('tok', 'grp'), may hold values from -0.0625 to 0.0625
- membership: int32 [16, 256], P('tok'), may hold values from 0 to 1, as said below
Outputs:
- eigen_values: float32 [8192, 16, 512], P('grp', None, 'tok')
Inputs may be any that keep to these rules, and one draw needn't show every extreme that they name: `membership`: along each row u the numbers never fall and both 0 and 1 appear; each sequence holds 64 to 192 rows, and in every draw some sequence holds exactly 192.
All inputs are finite; a program needn't handle non-finite values.
Results may differ from a plain program's by a relative error of at most 0.0017.
Values may be sent and summed in bfloat16 or wider, within the bound.
A program may use at most 128 MiB of HBM per device.

v0:
```python
import jax
import jax.numpy as jnp
from jax import lax
from jax.sharding import PartitionSpec as P

SEQ_DEV = 2


def local(acts, grads, basis_in, basis_out, membership):
    acts_full, grads_full = (
        lax.all_gather(acts, "grp", axis=1, tiled=True),
        lax.all_gather(grads, "grp", axis=1, tiled=True),
    )
    rows = acts_full.shape[0]
    panel = basis_in.shape[1]
    rot_in = jnp.dot(
        acts_full,
        lax.all_gather(basis_in, "tok", axis=0, tiled=True),
        preferred_element_type=jnp.float32,
    )
    rot_out = jnp.dot(
        grads_full,
        lax.all_gather(basis_out, "tok", axis=0, tiled=True),
        preferred_element_type=jnp.float32,
    )
    rot_in = rot_in.astype(jnp.bfloat16)
    rot_out = rot_out.astype(jnp.bfloat16)
    blocks = lax.axis_size("tok")
    part = panel // blocks
    seq_ids = jnp.arange(SEQ_DEV, dtype=jnp.int32)
    labels = membership[0]
    chosen = labels[None, :] == seq_ids[:, None]
    masked = jnp.where(chosen[:, :, None], rot_in[None, :, :], jnp.zeros((), jnp.bfloat16))
    slices = lax.all_to_all(masked, "tok", split_axis=2, concat_axis=1, tiled=True)
    every_rot_out = lax.all_gather(rot_out, "tok", axis=0, tiled=True)
    blocks_out = every_rot_out.reshape(blocks, rows, panel)
    piece = lax.all_gather(slices[None], "grp", axis=0, tiled=True)
    count = piece.shape[0]
    split = piece.reshape(count, SEQ_DEV, blocks, rows, part)
    moment = jnp.einsum("urp,qkurc->qkupc", blocks_out, split, preferred_element_type=jnp.float32)
    energy = jnp.sum(moment * moment, axis=(1, 2))
    energy = jnp.transpose(energy, (1, 0, 2))
    return energy / jnp.float32(rows * blocks)


def solution(mesh):
    placed = (P("tok", "grp"), P("tok", "grp"), P("tok", "grp"), P("tok", "grp"), P("tok", None))
    return jax.shard_map(
        local, mesh=mesh, in_specs=placed, out_specs=P("grp", None, "tok"), check_vma=False
    )
```

profile of v0, /device:TPU:10, one launch (start us, length us, event | category | flops | bytes accessed | tf_op | source)
XLA Modules:
  0.0 540.0 jit_solution(8460639361727462472)
XLA Ops:
  6.5 0.0 all-gather.13.cloned.1.call-start
  6.5 0.7 all-gather.13.cloned.1.call-update
  7.3 0.0 all-gather.15.cloned.1.call-start
  7.3 0.7 all-gather.15.cloned.1.call-update
  8.0 0.0 all-gather.7.cloned.1.call-start
  8.1 0.7 all-gather.7.cloned.1.call-update
  8.7 0.0 all-gather.9.cloned.1.call-start
  8.8 0.5 all-gather.9.cloned.1.call-update
  9.3 0.0 copy-start
  9.3 0.0 all-gather.17.cloned.1.call-start
  9.4 41.6 %all-gather.13.cloned.1.call-done = bf16[256,8192]{1,0:T(8,128)(2,1)} async-done(((bf16[256,512]{1,0:T(8,128)(2,1)}), bf16[256,8192]{1,0:T(8,128)(2,1)}) %all-gather.13.cloned.1.call-update) | async-done | bytes 4194320 | tf_op jit(solution)/shard_map/all_gather | solution.py:12
  51.0 138.6 %all-gather.15.cloned.1.call-done = bf16[8192,512]{1,0:T(8,128)(2,1)} async-done(((bf16[512,512]{1,0:T(8,128)(2,1)}), bf16[8192,512]{1,0:T(8,128)(2,1)}) %all-gather.15.cloned.1.call-update) | async-done | bytes 8388624 | tf_op jit(solution)/shard_map/all_gather | solution.py:23
  189.6 7.7 %convolution_convert_fusion = bf16[256,512]{1,0:T(8,128)(2,1)} fusion(bf16[256,8192]{1,0:T(8,128)(2,1)} %all-gather.13.cloned.1.call-done, bf16[8192,512]{1,0:T(8,128)(2,1)} %all-gather.15.cloned.1.call-done), kind=kOutput, calls=%fused_computation.3 | convolution fusion | flops 2147614720 | bytes 12845056 | tf_op jit(solution)/shard_map/dot_general | solution.py:21
  197.3 0.0 all-gather.17.cloned.1.call-update
  197.3 0.0 all-gather.11.cloned.1.call-start
  197.4 0.0 copy-done
  197.4 30.6 %all-gather.7.cloned.1.call-done = bf16[256,8192]{1,0:T(8,128)(2,1)} async-done(((bf16[256,512]{1,0:T(8,128)(2,1)}), bf16[256,8192]{1,0:T(8,128)(2,1)}) %all-gather.7.cloned.1.call-update) | async-done | bytes 4194320 | tf_op jit(solution)/shard_map/all_gather | solution.py:11
  228.0 138.5 %all-gather.9.cloned.1.call-done = bf16[8192,512]{1,0:T(8,128)(2,1)} async-done(((bf16[512,512]{1,0:T(8,128)(2,1)}), bf16[8192,512]{1,0:T(8,128)(2,1)}) %all-gather.9.cloned.1.call-update) | async-done | bytes 8388624 | tf_op jit(solution)/shard_map/all_gather | solution.py:18
  366.5 7.0 %convolution_convert_fusion.1 = bf16[256,512]{1,0:T(8,128)(2,1)S(1)} fusion(bf16[256,8192]{1,0:T(8,128)(2,1)} %all-gather.7.cloned.1.call-done, bf16[8192,512]{1,0:T(8,128)(2,1)} %all-gather.9.cloned.1.call-done), kind=kOutput, calls=%fused_computation.4 | convolution fusion | flops 2147614720 | bytes 12845056 | tf_op jit(solution)/shard_map/dot_general | solution.py:16
  373.5 0.1 copy.9
  373.6 0.5 broadcast_select_fusion
  374.2 28.8 %all_to_all.15 = bf16[2,256,512]{1,0,2:T(2,128)(2,1)S(1)} all-to-all(bf16[2,256,512]{1,0,2:T(2,128)(2,1)S(1)} %broadcast_select_fusion), channel_id=1, replica_groups=mesh['grp'=16,'tok'=16] {'tok'}, dimensions={2} | all-to-all | bytes 1048576 | tf_op jit(solution)/shard_map/all_to_all | solution.py:34
  403.0 0.1 copy.10
  403.1 0.3 copy.11
  403.4 1.0 broadcast_in_dim.29
  404.4 0.0 all-gather.11.cloned.1.call-update
  404.5 65.6 %all-gather.17.cloned.1.call-done = bf16[4096,512]{1,0:T(8,128)(2,1)} async-done(((bf16[256,512]{1,0:T(8,128)(2,1)}), bf16[4096,512]{1,0:T(8,128)(2,1)}) %all-gather.17.cloned.1.call-update) | async-done | bytes 4194320 | tf_op jit(solution)/shard_map/all_gather | solution.py:35
  470.0 53.8 %all-gather.11.cloned.1.call-done = bf16[16,2,4096,32]{2,3,1,0:T(8,128)(2,1)} async-done(((bf16[1,2,4096,32]{2,3,1,0:T(8,128)(2,1)}), bf16[16,2,4096,32]{2,3,1,0:T(8,128)(2,1)}) %all-gather.11.cloned.1.call-update) | async-done | bytes 8388624 | tf_op jit(solution)/shard_map/all_gather | solution.py:37
  523.8 8.3 %multiply_reduce_fusion = f32[16,32,512]{2,1,0:T(8,128)S(1)} fusion(bf16[16,256,512,1,1]{2,1,4,3,0:T(8,128)(2,1)} %bitcast.27, bf16[16,2,4,16,8,256]{5,4,3,2,1,0:T(8,128)(2,1)} %bitcast.26), kind=kOutput, calls=%fused_computation | convolution fusion | flops 4311482368 | bytes 13631488 | tf_op jit(solution)/shard_map/urp,qkurc->qkupc/dot_general | solution.py:40
  532.1 1.1 multiply_bitcast_fusion
  (1 shorter events, 0.0 us)
Async XLA Ops:
  6.5 44.4 %all-gather.13.cloned.1.call-start = ((), (), s32[]{:S(2)}) async-start(), calls=%async_computation.4 | async-start | bytes 4456448 | tf_op jit(solution)/shard_map/all_gather | solution.py:12
  7.3 182.3 %all-gather.15.cloned.1.call-start = ((), (), s32[]{:S(2)}) async-start(), calls=%async_computation.5 | async-start | bytes 8912896 | tf_op jit(solution)/shard_map/all_gather | solution.py:23
  8.0 220.0 %all-gather.7.cloned.1.call-start = ((), (), s32[]{:S(2)}) async-start(), calls=%async_computation.1 | async-start | bytes 4456448 | tf_op jit(solution)/shard_map/all_gather | solution.py:11
  8.7 357.8 %all-gather.9.cloned.1.call-start = ((), (), s32[]{:S(2)}) async-start(), calls=%async_computation.2 | async-start | bytes 8912896 | tf_op jit(solution)/shard_map/all_gather | solution.py:18
  9.3 188.0 %copy-start = (s32[1,256]{1,0:T(1,128)S(1)}, s32[1,256]{1,0:T(1,128)}, u32[]{:S(2)}) copy-start(s32[1,256]{1,0:T(1,128)} %param.9) | copy-start | bytes 3076
  9.3 460.7 %all-gather.17.cloned.1.call-start = ((), (), s32[]{:S(2)}) async-start(), calls=%async_computation.6 | async-start | bytes 4456448 | tf_op jit(solution)/shard_map/all_gather | solution.py:35
  197.3 326.5 %all-gather.11.cloned.1.call-start = ((), (), s32[]{:S(2)}) async-start(), calls=%async_computation.3 | async-start | bytes 8912896 | tf_op jit(solution)/shard_map/all_gather | solution.py:37
Sparse Core Ops, SparseCore 0:
  9.2 41.7 all-gather.12
  53.6 135.9 all-gather.14
  191.4 36.5 all-gather.6
  230.5 135.9 all-gather.8
  368.9 101.0 all-gather.16
  471.7 52.0 all-gather.10
where the time goes:
time: 541 us; the launch traced here: 540 us
  waiting for transfers between devices  471 us (87%)
  blocking collectives  28.8 us (5%)
  matrix products  22.9 us (4%)
  between operations  13.5 us (2%)
    all_gather x1, waiting for transfers between devices, local(): lax.all_gather(basis_out, 'tok', axis=0, tiled=True)  139 us
    all_gather x1, waiting for transfers between devices, local(): lax.all_gather(basis_in, 'tok', axis=0, tiled=True)  138 us
    all_gather x1, waiting for transfers between devices, local(): every_rot_out = lax.all_gather(rot_out, 'tok', axis=0, tiled=True)  65.6 us
    all_gather x1, waiting for transfers between devices, local(): piece = lax.all_gather(slices[None], 'grp', axis=0, tiled=True)  53.8 us
    all_gather x1, waiting for transfers between devices, local(): lax.all_gather(grads, 'grp', axis=1, tiled=True)  41.6 us
    all_gather x1, waiting for transfers between devices, local(): lax.all_gather(acts, 'grp', axis=1, tiled=True)  30.6 us
    all_to_all x1, blocking collectives, local(): lax.all_to_all(masked, 'tok', split_axis=2, concat_axis=1, tiled=True)  28.8 us
  transfers between devices with their start and end apart: 6, of which 6 were waited for; matrix products, arithmetic and copies ran while one was open for 3% of the time, Pallas kernels for 0%

commit v1 on v0

v1 whole, which is shorter than its diff:
```python
import jax
import jax.numpy as jnp
from jax import lax
from jax.experimental import pallas as pl
from jax.experimental.pallas import tpu as pltpu
from jax.sharding import PartitionSpec as P

MESH = pl.DeviceIdType.MESH
F32, BF16 = jnp.float32, jnp.bfloat16
NSEM = 160


def kernel(acts, grads, basis_in, basis_out, own_labels, out, a_buf, b_buf, part, landed, rot_out,
           rin_send, rot_in, labels, ssem, rsem, lsem):
    g, t = lax.axis_index("grp"), lax.axis_index("tok")
    c, x, yl = lax.rem(g, 2), lax.rem(lax.div(g, 2), 4), lax.div(g, 8)
    z, yh = lax.div(t, 2), lax.rem(t, 2)

    def grp(x_, yl_, c_):
        return (yl_ * 4 + x_) * 2 + c_

    def xat(step):
        return lax.rem(x + 4 + step, 4)

    def zat(step):
        return lax.rem(z + 8 + step, 8)

    to_x = {1: {"grp": grp(xat(1), yl, c)}, -1: {"grp": grp(xat(-1), yl, c)}}
    to_z = {1: {"tok": zat(1) * 2 + yh}, -1: {"tok": zat(-1) * 2 + yh}}
    to_yl = {"grp": grp(x, 1 - yl, c)}
    to_yh = {"tok": z * 2 + 1 - yh}
    to_sib = {"grp": grp(x, yl, 1 - c)}
    to_diag = {"grp": grp(x, yl, 1 - c), "tok": z * 2 + 1 - yh}
    to_tok = [None] + [{"tok": lax.rem(t + d, 16)} for d in range(1, 16)]

    barrier = pltpu.get_barrier_semaphore()
    partners = to_tok[1:] + [to_diag, to_x[1], to_x[-1], to_yl, to_sib]
    for partner in partners:
        pl.semaphore_signal(barrier, inc=1, device_id=partner, device_id_type=MESH)
    pl.semaphore_wait(barrier, len(partners))

    used = [0]
    sent = []

    def make(src, dst, dev):
        at = used[0]
        used[0] += 1
        return pltpu.make_async_remote_copy(
            src_ref=src, dst_ref=dst, send_sem=ssem.at[at], recv_sem=rsem.at[at],
            device_id=dev, device_id_type=MESH)

    def send(src, dst, dev):
        copy = make(src, dst, dev)
        copy.start()
        sent.append(copy)
        return copy

    feats, bases = (acts, grads), (basis_in, basis_out)

    ring = {}

    def half_of(d, first):
        return 0 if (d == 1) == first else 1

    def b_send(m, s, first):
        for d in (1, -1):
            if s == 4 and not first:
                continue
            rows = pl.ds(half_of(d, first) * 256, 256)
            block = zat(-(s - 1) * d)
            src = bases[m].at[rows] if s == 1 else b_buf.at[m, block, rows]
            ring[m, s, first, d] = send(src, b_buf.at[m, block, rows], to_z[d])

    def b_wait(m, s, first):
        for d in (1, -1):
            ring[m, s, first, d].wait_recv()

    def b_pass(m, s, first):
        b_wait(m, s, first)
        b_send(m, s + 1, first)

    b_send(0, 1, True)
    b_send(0, 1, False)

    diag = [make(feats[m], a_buf.at[m, yh, x, yl], to_diag) for m in range(2)]
    stay = [pltpu.make_async_copy(feats[m], a_buf.at[m, yh, x, yl], lsem.at[m]) for m in range(2)]
    keep = [pltpu.make_async_copy(bases[m], b_buf.at[m, z], lsem.at[2 + m]) for m in range(2)]

    @pl.when(yh != c)
    def _():
        for m in range(2):
            diag[m].start()

    @pl.when(yh == c)
    def _():
        for m in range(2):
            stay[m].start()

    for copy in keep:
        copy.start()
    label_copies = [None]
    for d in range(1, 16):
        label_copies.append(send(own_labels, labels.at[t], to_tok[d]))
    labels[t] = own_labels[...]
    part[...] = jnp.zeros_like(part)
    out[...] = jnp.zeros_like(out)

    feat = {}

    def a_diag_wait(m):
        @pl.when(yh != c)
        def _():
            diag[m].wait()

        @pl.when(yh == c)
        def _():
            stay[m].wait()

    def a_yl(m):
        mine = a_buf.at[m, c, x, yl]
        feat[m, "yl"] = send(mine, mine, to_yl)

    def a_x1(m):
        feat[m, "yl"].wait_recv()
        mine = a_buf.at[m, c, x]
        for d in (1, -1):
            feat[m, "x1", d] = send(mine, mine, to_x[d])

    def a_x2(m):
        for d in (1, -1):
            feat[m, "x1", d].wait_recv()
        for d, lane in ((1, 0), (-1, 1)):
            moved = a_buf.at[m, c, xat(-d), lane]
            feat[m, "x2", d] = send(moved, moved, to_x[d])

    def a_sib(m):
        for d in (1, -1):
            feat[m, "x2", d].wait_recv()
        mine = a_buf.at[m, c]
        feat[m, "sib"] = send(mine, mine, to_sib)

    def multiply(m, block):
        xb, yb = lax.rem(block, 4), lax.div(block, 4)
        for half in range(2):
            part[m, half] += jnp.dot(a_buf[m, half, xb, yb], b_buf[m, block], preferred_element_type=F32)

    def multiply_near(m, lo, hi):
        @pl.loop(lo, hi)
        def _(step):
            multiply(m, lax.rem(z + 8 + step, 8))

    def multiply_pair(m, step):
        @pl.loop(0, 2)
        def _(way):
            multiply(m, lax.rem(z + 8 + step * (1 - 2 * way), 8))

    reduce = {}

    def r_send(m, nh):
        cols = pl.ds(nh * 256, 256)
        reduce[m, nh] = send(part.at[m, 1 - yh, :, cols], landed.at[m, :, cols], to_yh)

    def rotated(m, nh):
        reduce[m, nh].wait_recv()
        cols = pl.ds(nh * 256, 256)
        total = part[m, yh, :, cols] + landed[m, :, cols]
        return jnp.transpose(total).astype(BF16)

    rin = {}

    def i_slices():
        for nh in range(2):
            rin_send[pl.ds(nh * 8, 8)] = rotated(0, nh).reshape(8, 32, 256)
        for d in range(1, 16):
            rin[d] = send(rin_send.at[lax.rem(t + d, 16)], rot_in.at[x, yl, c, t], to_tok[d])
        rot_in[x, yl, c, t] = rin_send[t]

    def i_yl():
        for d in range(1, 16):
            rin[d].wait_recv()
        mine = rot_in.at[x, yl, c]
        rin["yl"] = send(mine, mine, to_yl)

    def i_x1():
        rin["yl"].wait_recv()
        mine = rot_in.at[x, :, c]
        for d in (1, -1):
            rin["x1", d] = send(mine, mine, to_x[d])

    def i_x2():
        for d in (1, -1):
            rin["x1", d].wait_recv()
        for d, lane in ((1, 0), (-1, 1)):
            moved = rot_in.at[xat(-d), lane, c]
            rin["x2", d] = send(moved, moved, to_x[d])

    def i_sib():
        for d in (1, -1):
            rin["x2", d].wait_recv()
        mine = rot_in.at[:, :, c]
        rin["sib"] = send(mine, mine, to_sib)

    a_diag_wait(0)
    a_yl(0)
    b_pass(0, 1, True)
    a_diag_wait(1)
    a_yl(1)
    a_x1(0)
    b_pass(0, 1, False)
    b_pass(0, 2, True)
    a_x2(0)
    b_pass(0, 2, False)
    a_sib(0)
    a_x1(1)
    b_pass(0, 3, True)
    for copy in keep:
        copy.wait()
    feat[0, "sib"].wait_recv()
    multiply_near(0, -2, 3)
    b_wait(0, 3, False)
    b_send(1, 1, True)
    b_send(1, 1, False)
    multiply_pair(0, 3)
    b_wait(0, 4, True)
    multiply(0, zat(4))
    r_send(0, 0)
    r_send(0, 1)
    a_x2(1)
    b_pass(1, 1, True)
    a_sib(1)
    b_pass(1, 1, False)
    i_slices()
    feat[1, "sib"].wait_recv()
    multiply_near(1, -1, 2)
    b_pass(1, 2, True)
    i_yl()
    b_pass(1, 2, False)
    multiply_pair(1, 2)
    i_x1()
    b_pass(1, 3, True)
    i_x2()
    b_wait(1, 3, False)
    multiply_pair(1, 3)
    b_wait(1, 4, True)
    multiply(1, zat(4))
    r_send(1, 1)
    r_send(1, 0)
    i_sib()

    low, high = pl.ds(0, 256), pl.ds(256, 256)
    gat = {}

    def o_single(s):
        for d in (1, -1):
            block = 2 * zat(-(s - 1) * d) + yh
            rows = high if s < 4 else pl.ds(256 if d == 1 else 384, 128)
            ref = rot_out.at[block, rows]
            gat["s", s, d] = send(ref, ref, to_z[d])

    def o_cross(s):
        for d in ((1, -1) if s in (1, 2, 3) else (1,)):
            ref = rot_out.at[2 * zat(-s * d) + yh, high]
            gat["c", s, d] = send(ref, ref, to_yh)

    def o_pair(s):
        for d in (1, -1):
            block = zat(-(s - 1) * d)
            ref = rot_out.at[pl.ds(2 * block, 2), low] if s < 4 else rot_out.at[2 * block + (d < 0), low]
            gat["p", s, d] = send(ref, ref, to_z[d])

    def o_wait(kind, s):
        for d in (1, -1):
            if (kind, s, d) in gat:
                gat[kind, s, d].wait_recv()

    rot_out[t, high] = rotated(1, 1)
    o_single(1)
    o_cross(0)
    rot_out[t, low] = rotated(1, 0)
    ref = rot_out.at[t, low]
    lower = send(ref, ref, to_yh)
    o_wait("s", 1)
    o_single(2)
    o_cross(1)
    lower.wait_recv()
    o_pair(1)
    o_wait("s", 2)
    o_single(3)
    o_cross(2)
    o_wait("p", 1)
    o_pair(2)
    o_wait("s", 3)
    o_single(4)
    o_cross(3)
    o_wait("p", 2)
    o_pair(3)

    def moments(u):
        mine = rot_in[:, :, :, u].reshape(512, 256)
        second = labels[u][0:1].astype(BF16)
        for keep_mask in (second, 1.0 - second):
            masked = mine * keep_mask
            for half in range(2):
                rows = pl.ds(half * 256, 256)
                moment = lax.dot_general(rot_out[u, rows], masked, (((1,), (1,)), ((), ())),
                                         preferred_element_type=F32)
                out[rows] += moment * moment

    def moments_at(step):
        @pl.loop(0, 2)
        def _(j):
            moments(2 * lax.rem(z + 8 + step, 8) + j)

    for d in range(1, 16):
        label_copies[d].wait_recv()
    rin["sib"].wait_recv()
    o_wait("c", 0)
    moments_at(0)
    o_wait("s", 4)
    o_cross(4)
    o_wait("p", 3)
    o_pair(4)
    for s in (1, 2, 3):
        o_wait("c", s)
        moments_at(s)
        moments_at(-s)
    o_wait("p", 4)
    o_wait("c", 4)
    moments_at(4)
    out[...] = out[...] * F32(1.0 / 4096)
    for copy in sent:
        copy.wait_send()


def local(acts, grads, basis_in, basis_out, membership):
    own_labels = jnp.broadcast_to(membership, (8, 256)).astype(F32)
    any_space, vmem = pl.BlockSpec(memory_space=pl.ANY), pl.BlockSpec(memory_space=pltpu.VMEM)
    energy = pl.pallas_call(
        kernel,
        out_shape=jax.ShapeDtypeStruct((512, 512), F32),
        in_specs=[any_space] * 4 + [vmem],
        out_specs=vmem,
        scratch_shapes=[
            pltpu.VMEM((2, 2, 4, 2, 256, 512), BF16),
            pltpu.VMEM((2, 8, 512, 512), BF16),
            pltpu.VMEM((2, 2, 256, 512), F32),
            pltpu.VMEM((2, 256, 512), F32),
            pltpu.VMEM((16, 512, 256), BF16),
            pltpu.VMEM((16, 32, 256), BF16),
            pltpu.VMEM((4, 2, 2, 16, 32, 256), BF16),
            pltpu.VMEM((16, 8, 256), F32),
            pltpu.SemaphoreType.DMA((NSEM,)),
            pltpu.SemaphoreType.DMA((NSEM,)),
            pltpu.SemaphoreType.DMA((4,)),
        ],
        compiler_params=pltpu.CompilerParams(
            collective_id=0, has_side_effects=True, vmem_limit_bytes=56 * 1024 * 1024),
        name="ekfac",
    )(acts, grads, basis_in, basis_out, own_labels)
    return energy.reshape(512, 4, 2, 2, 32).transpose(0, 2, 1, 3, 4).reshape(512, 16, 32)


def solution(mesh):
    placed = (P("tok", "grp"), P("tok", "grp"), P("tok", "grp"), P("tok", "grp"), P("tok", None))
    return jax.shard_map(
        local, mesh=mesh, in_specs=placed, out_specs=P("grp", None, "tok"), check_vma=False
    )
```

time: 541 us -> 167 us (0.31)
  waiting for transfers between devices: 471 us -> 0 us
  Pallas kernels: 0 us -> 163 us
  blocking collectives: 28.8 us -> 0 us
  matrix products: 22.9 us -> 0 us
  between operations: 13.5 us -> 0.02 us
    all_gather x6 -> x0, waiting for transfers between devices: 469 us -> none  [the longest x1 139 us: local(): lax.all_gather(basis_out, 'tok', axis=0, tiled=True)]
    pallas_call x0 -> x1, Pallas kernels: none -> 163 us  [local(): pl.pallas_call(kernel, out_shape=jax.ShapeDtypeStruct((512, 512), F32), i...]
    all_to_all x1 -> x0, blocking collectives: 28.8 us -> none  [local(): lax.all_to_all(masked, 'tok', split_axis=2, concat_axis=1, tiled=True)]
    dot_general x3 -> x0, matrix products: 22.9 us -> none  [the longest x1 8.28 us: local(): jnp.einsum('urp,qkurc->qkupc', blocks_out, split, preferred_element_type=...]
  transfers between devices with their start and end apart: 6 -> 0, of which waited for: 6 -> 0; matrix products, arithmetic and copies ran while one was open for 3% -> 0% of each run, Pallas kernels for 0% -> 0%
where the time goes in v1:
time: 167 us
  Pallas kernels  163 us (98%)
  local copies, waits for them, and re-layouts  3.23 us (2%)
    pallas_call x1, Pallas kernels, local(): pl.pallas_call(kernel, out_shape=jax.ShapeDtypeStruct((512, 512), F32), i...  163 us

profile of v1, /device:TPU:10, one launch (start us, length us, event | category | flops | bytes accessed | tf_op | source)
XLA Modules:
  0.0 166.6 jit_solution(5186120873715508741)
XLA Ops:
  0.0 0.7 convert_element_type.5
  0.7 0.6 broadcast_in_dim.2.own_labels
  1.3 162.6 %ekfac.1 = f32[512,512]{1,0:T(8,128)} custom-call(bf16[256,512]{1,0:T(8,128)(2,1)} %acts.1, bf16[256,512]{1,0:T(8,128)(2,1)} %grads.1, bf16[512,512]{1,0:T(8,128)(2,1)} %basis_in.1, bf16[512,512]{1,0:T(8,128)(2,1)} %basis_out.1, f32[8,256]{1,0:T(8,128)} %broadcast_in_dim.2.own_labels), custom_call_target="tpu_custom_call" | custom-call | tf_op jit(solution)/shard_map/ekfac/pallas_call | solution.py:338
  163.9 1.6 copy.8
  165.5 1.1 copy.9

commit v2 on v1

v2 whole, which is shorter than its diff:
```python
import jax
import jax.numpy as jnp
from jax import lax
from jax.experimental import pallas as pl
from jax.experimental.pallas import tpu as pltpu
from jax.sharding import PartitionSpec as P

MESH = pl.DeviceIdType.MESH
F32, BF16 = jnp.float32, jnp.bfloat16
NSEM = 200


def kernel(acts, grads, basis_in, basis_out, membership, out, a_buf, b_buf, part, landed, rot_out,
           rin_send, rot_in, labels, ssem, rsem, lsem):
    g, t = lax.axis_index("grp"), lax.axis_index("tok")
    c, x, yl = lax.rem(g, 2), lax.rem(lax.div(g, 2), 4), lax.div(g, 8)
    z, yh = lax.div(t, 2), lax.rem(t, 2)

    def grp(x_, yl_, c_):
        return (yl_ * 4 + x_) * 2 + c_

    def xat(step):
        return lax.rem(x + 4 + step, 4)

    def zat(step):
        return lax.rem(z + 8 + step, 8)

    to_x = {1: {"grp": grp(xat(1), yl, c)}, -1: {"grp": grp(xat(-1), yl, c)}}
    to_z = {1: {"tok": zat(1) * 2 + yh}, -1: {"tok": zat(-1) * 2 + yh}}
    to_yl = {"grp": grp(x, 1 - yl, c)}
    to_yh = {"tok": z * 2 + 1 - yh}
    to_sib = {"grp": grp(x, yl, 1 - c)}
    to_diag = {"grp": grp(x, yl, 1 - c), "tok": z * 2 + 1 - yh}
    to_tok = [None] + [{"tok": lax.rem(t + d, 16)} for d in range(1, 16)]

    barrier = pltpu.get_barrier_semaphore()
    partners = to_tok[1:] + [to_diag, to_x[1], to_x[-1], to_yl, to_sib]
    for partner in partners:
        pl.semaphore_signal(barrier, inc=1, device_id=partner, device_id_type=MESH)
    pl.semaphore_wait(barrier, len(partners))

    used = [0]
    sent = []

    def make(src, dst, dev):
        at = used[0]
        used[0] += 1
        return pltpu.make_async_remote_copy(
            src_ref=src, dst_ref=dst, send_sem=ssem.at[at], recv_sem=rsem.at[at],
            device_id=dev, device_id_type=MESH)

    def send(src, dst, dev):
        copy = make(src, dst, dev)
        copy.start()
        sent.append(copy)
        return copy

    feats, bases = (acts, grads), (basis_in, basis_out)

    ring = {}

    def b_part(k, block, first, d):
        half = 0 if (d == 1) == first else 1
        if k == 0:
            cols = pl.ds(half * 256, 256)
            return basis_in.at[:, cols], b_buf.at[0, half, block]
        rows, cols = pl.ds(half * 256, 256), pl.ds((k - 1) * 256, 256)
        return basis_out.at[rows, cols], b_buf.at[1, k - 1, block, rows]

    def b_send(k, s, first):
        for d in (1, -1):
            if s == 4 and not first:
                continue
            source, slot = b_part(k, zat(-(s - 1) * d), first, d)
            ring[k, s, first, d] = send(source if s == 1 else slot, slot, to_z[d])

    def b_wait(k, s, first):
        for d in (1, -1):
            ring[k, s, first, d].wait_recv()

    def b_pass(k, s, first):
        b_wait(k, s, first)
        b_send(k, s + 1, first)

    b_send(0, 1, True)
    b_send(0, 1, False)

    diag = [make(feats[m], a_buf.at[m, yh, x, yl], to_diag) for m in range(2)]
    stay = [pltpu.make_async_copy(feats[m], a_buf.at[m, yh, x, yl], lsem.at[m]) for m in range(2)]
    keep = [pltpu.make_async_copy(bases[m].at[:, pl.ds(nh * 256, 256)], b_buf.at[m, nh, z], lsem.at[2 + 2 * m + nh])
            for m in range(2) for nh in range(2)]

    @pl.when(yh != c)
    def _():
        for m in range(2):
            diag[m].start()

    @pl.when(yh == c)
    def _():
        for m in range(2):
            stay[m].start()

    for copy in keep:
        copy.start()
    labels[t] = membership[...]
    mine = labels.at[t]
    label_copies = [None] + [send(mine, mine, to_tok[d]) for d in range(1, 16)]
    part[...] = jnp.zeros_like(part)
    out[...] = jnp.zeros_like(out)

    feat = {}

    def a_diag_wait(m):
        @pl.when(yh != c)
        def _():
            diag[m].wait()

        @pl.when(yh == c)
        def _():
            stay[m].wait()

    def a_own(m):
        a_diag_wait(m)
        mine = a_buf.at[m, c, x, yl]
        feat[m, "yl"] = send(mine, mine, to_yl)
        for d in (1, -1):
            feat[m, "own", d] = send(mine, mine, to_x[d])

    def a_other(m):
        feat[m, "yl"].wait_recv()
        theirs = a_buf.at[m, c, x, 1 - yl]
        for d in (1, -1):
            feat[m, "other", d] = send(theirs, theirs, to_x[d])

    def a_x2(m):
        for d in (1, -1):
            feat[m, "own", d].wait_recv()
            feat[m, "other", d].wait_recv()
        for d, lane in ((1, 0), (-1, 1)):
            moved = a_buf.at[m, c, xat(-d), lane]
            feat[m, "x2", d] = send(moved, moved, to_x[d])

    def a_sib(m):
        for d in (1, -1):
            feat[m, "x2", d].wait_recv()
        mine = a_buf.at[m, c]
        feat[m, "sib"] = send(mine, mine, to_sib)

    def multiply(m, halves, block):
        xb, yb = lax.rem(block, 4), lax.div(block, 4)
        for nh in halves:
            for half in range(2):
                part[m, nh, half] += jnp.dot(
                    a_buf[m, half, xb, yb], b_buf[m, nh, block], preferred_element_type=F32)

    def multiply_near(m, halves, lo, hi):
        @pl.loop(lo, hi)
        def _(step):
            multiply(m, halves, lax.rem(z + 8 + step, 8))

    def multiply_pair(m, halves, step):
        @pl.loop(0, 2)
        def _(way):
            multiply(m, halves, lax.rem(z + 8 + step * (1 - 2 * way), 8))

    reduce = {}

    def r_send(m, nh, lo=0, size=256):
        cols = pl.ds(lo, size)
        reduce[m, nh, lo] = send(part.at[m, nh, 1 - yh, :, cols], landed.at[m, nh, :, cols], to_yh)

    def rotated(m, nh, lo=0, size=256):
        reduce[m, nh, lo].wait_recv()
        cols = pl.ds(lo, size)
        return jnp.transpose(part[m, nh, yh, :, cols] + landed[m, nh, :, cols]).astype(BF16)

    rin = {}

    def i_slices():
        for nh in range(2):
            rin_send[pl.ds(nh * 8, 8)] = rotated(0, nh).reshape(8, 32, 256)
        for d in range(1, 16):
            rin[d] = send(rin_send.at[lax.rem(t + d, 16)], rot_in.at[x, yl, c, t], to_tok[d])
        rot_in[x, yl, c, t] = rin_send[t]

    def i_own():
        for d in range(1, 16):
            rin[d].wait_recv()
        mine = rot_in.at[x, yl, c]
        rin["yl"] = send(mine, mine, to_yl)
        for d in (1, -1):
            rin["own", d] = send(mine, mine, to_x[d])

    def i_other():
        rin["yl"].wait_recv()
        theirs = rot_in.at[x, 1 - yl, c]
        for d in (1, -1):
            rin["other", d] = send(theirs, theirs, to_x[d])

    def i_x2():
        for d in (1, -1):
            rin["own", d].wait_recv()
            rin["other", d].wait_recv()
        for d, lane in ((1, 0), (-1, 1)):
            moved = rot_in.at[xat(-d), lane, c]
            rin["x2", d] = send(moved, moved, to_x[d])

    def i_sib():
        for d in (1, -1):
            rin["x2", d].wait_recv()
        mine = rot_in.at[:, :, c]
        rin["sib"] = send(mine, mine, to_sib)

    gat = {}
    chains = {0: (0, 256, 0), 1: (256, 128, 128)}

    def o_send(key, ref, dev):
        gat[key] = send(ref, ref, dev)

    def o_start(nh):
        lo, size, _ = chains[nh]
        rot_out[t, pl.ds(lo, size)] = rotated(1, nh, 0, size)
        o_single(nh, 1)
        o_cross(nh, 0)

    def o_start_pair(nh):
        lo, single, size = chains[nh]
        rows = pl.ds(lo + single, size)
        rot_out[t, rows] = rotated(1, nh, single, size)
        o_send((nh, "y"), rot_out.at[t, rows], to_yh)

    def o_single(nh, s):
        lo, size, _ = chains[nh]
        for d in (1, -1):
            block = 2 * zat(-(s - 1) * d) + yh
            rows = pl.ds(lo, size) if s < 4 else pl.ds(lo if d == 1 else lo + size // 2, size // 2)
            o_send((nh, "s", s, d), rot_out.at[block, rows], to_z[d])

    def o_cross(nh, s):
        lo, size, _ = chains[nh]
        for d in ((1, -1) if s in (1, 2, 3) else (1,)):
            o_send((nh, "c", s, d), rot_out.at[2 * zat(-s * d) + yh, pl.ds(lo, size)], to_yh)

    def o_pair(nh, s):
        lo, single, size = chains[nh]
        rows = pl.ds(lo + single, size)
        for d in (1, -1):
            block = zat(-(s - 1) * d)
            ref = rot_out.at[pl.ds(2 * block, 2), rows] if s < 4 else rot_out.at[2 * block + (d < 0), rows]
            o_send((nh, "p", s, d), ref, to_z[d])

    def o_wait(nh, kind, s):
        for d in (1, -1):
            if (nh, kind, s, d) in gat:
                gat[nh, kind, s, d].wait_recv()

    def o_pass(nh, s):
        o_wait(nh, "s", s)
        if s < 4:
            o_single(nh, s + 1)
        o_cross(nh, s)

    def o_pass_pair(nh, s):
        if s == 0:
            gat[nh, "y"].wait_recv()
        else:
            o_wait(nh, "p", s)
        o_pair(nh, s + 1)

    def moments(nh, blocks):
        for yb in range(2):
            total = None
            for u in blocks:
                second = labels[u].astype(F32).astype(BF16)
                weights = rot_out[u, pl.ds(nh * 256, 256)]
                mine = rot_in[:, yb, :, u].reshape(256, 256)
                for keep_mask in (second, 1.0 - second):
                    moment = lax.dot_general(mine * keep_mask, weights, (((1,), (1,)), ((), ())),
                                             preferred_element_type=F32)
                    moment = moment * moment
                    total = moment if total is None else total + moment
            out[pl.ds(yb * 256, 256), pl.ds(nh * 256, 256)] += total

    def moments_at(nh, s):
        o_wait(nh, "c", s)
        blocks = []
        for step in ((s,) if s in (0, 4) else (s, -s)):
            block = 2 * zat(step)
            blocks += [block, block + 1]
        moments(nh, blocks)

    n0, n1, both_halves = (0,), (1,), (0, 1)
    a_own(0)
    b_pass(0, 1, True)
    b_pass(0, 1, False)
    a_other(0)
    b_pass(0, 2, True)
    a_x2(0)
    a_own(1)
    b_pass(0, 2, False)
    a_sib(0)
    a_other(1)
    for copy in keep:
        copy.wait()
    b_pass(0, 3, True)
    feat[0, "sib"].wait_recv()
    multiply_near(0, both_halves, -2, 3)
    b_wait(0, 3, False)
    b_send(1, 1, True)
    b_send(1, 1, False)
    multiply_pair(0, both_halves, 3)
    a_x2(1)
    b_wait(0, 4, True)
    multiply(0, both_halves, zat(4))
    r_send(0, 0)
    r_send(0, 1)
    b_pass(1, 1, True)
    a_sib(1)
    b_pass(1, 1, False)
    b_pass(1, 2, True)
    b_pass(1, 2, False)
    feat[1, "sib"].wait_recv()
    b_pass(1, 3, True)
    multiply_near(1, n0, -1, 2)
    b_wait(1, 3, False)
    b_send(2, 1, True)
    b_send(2, 1, False)
    i_slices()
    multiply_pair(1, n0, 2)
    b_wait(1, 4, True)
    multiply_pair(1, n0, 3)
    multiply(1, n0, zat(4))
    r_send(1, 0)
    b_pass(2, 1, True)
    b_pass(2, 1, False)
    i_own()
    b_pass(2, 2, True)
    b_pass(2, 2, False)
    o_start(0)
    multiply_near(1, n1, -1, 2)
    i_other()
    b_pass(2, 3, True)
    o_pass(0, 1)
    b_wait(2, 3, False)
    multiply_pair(1, n1, 2)
    multiply_pair(1, n1, 3)
    i_x2()
    b_wait(2, 4, True)
    multiply(1, n1, zat(4))
    r_send(1, 1, 128, 128)
    r_send(1, 1, 0, 128)
    o_pass(0, 2)
    i_sib()
    o_start_pair(1)
    o_start(1)
    o_pass(0, 3)
    for d in range(1, 16):
        label_copies[d].wait_recv()
    o_pass_pair(1, 0)
    o_pass(0, 4)
    o_pass(1, 1)
    rin["sib"].wait_recv()
    moments_at(0, 0)
    o_pass_pair(1, 1)
    o_pass(1, 2)
    moments_at(0, 1)
    o_pass_pair(1, 2)
    o_pass(1, 3)
    moments_at(0, 2)
    o_pass_pair(1, 3)
    o_pass(1, 4)
    moments_at(0, 3)
    moments_at(0, 4)
    moments_at(1, 0)
    moments_at(1, 1)
    moments_at(1, 2)
    moments_at(1, 3)
    o_wait(1, "p", 4)
    moments_at(1, 4)
    out[...] = out[...] * F32(1.0 / 4096)
    for copy in sent:
        copy.wait_send()


def local(acts, grads, basis_in, basis_out, membership):
    any_space, vmem = pl.BlockSpec(memory_space=pl.ANY), pl.BlockSpec(memory_space=pltpu.VMEM)
    energy = pl.pallas_call(
        kernel,
        out_shape=jax.ShapeDtypeStruct((512, 512), F32),
        in_specs=[any_space] * 4 + [vmem],
        out_specs=vmem,
        scratch_shapes=[
            pltpu.VMEM((2, 2, 4, 2, 256, 512), BF16),
            pltpu.VMEM((2, 2, 8, 512, 256), BF16),
            pltpu.VMEM((2, 2, 2, 256, 256), F32),
            pltpu.VMEM((2, 2, 256, 256), F32),
            pltpu.VMEM((16, 512, 256), BF16),
            pltpu.VMEM((16, 32, 256), BF16),
            pltpu.VMEM((4, 2, 2, 16, 32, 256), BF16),
            pltpu.VMEM((16, 1, 256), jnp.int32),
            pltpu.SemaphoreType.DMA((NSEM,)),
            pltpu.SemaphoreType.DMA((NSEM,)),
            pltpu.SemaphoreType.DMA((6,)),
        ],
        compiler_params=pltpu.CompilerParams(
            collective_id=0, has_side_effects=True, vmem_limit_bytes=56 * 1024 * 1024),
        name="ekfac",
    )(acts, grads, basis_in, basis_out, membership)
    return jnp.transpose(energy.reshape(16, 32, 512), (2, 0, 1))


def solution(mesh):
    placed = (P("tok", "grp"), P("tok", "grp"), P("tok", "grp"), P("tok", "grp"), P("tok", None))
    return jax.shard_map(
        local, mesh=mesh, in_specs=placed, out_specs=P("grp", None, "tok"), check_vma=False
    )
```

time: 167 us -> 147 us (0.88)
  Pallas kernels: 163 us -> 144 us
    pallas_call x1, Pallas kernels: 163 us -> 144 us  [local(): pl.pallas_call(kernel, out_shape=jax.ShapeDtypeStruct((512, 512), F32), i...]
    unnamed x0 -> x1, local copies, waits for them, and re-layouts: none -> 2.29 us
where the time goes in v2:
time: 147 us; the launch traced here: 146 us
  Pallas kernels  144 us (98%)
  local copies, waits for them, and re-layouts  2.29 us (2%)
    pallas_call x1, Pallas kernels, local(): pl.pallas_call(kernel, out_shape=jax.ShapeDtypeStruct((512, 512), F32), i...  144 us

profile of v2, /device:TPU:10, one launch (start us, length us, event | category | flops | bytes accessed | tf_op | source)
XLA Modules:
  0.0 146.2 jit_solution(14071131134695458808)
XLA Ops:
  0.0 143.9 %ekfac.1 = f32[512,512]{1,0:T(8,128)} custom-call(bf16[256,512]{1,0:T(8,128)(2,1)} %acts.1, bf16[256,512]{1,0:T(8,128)(2,1)} %grads.1, bf16[512,512]{1,0:T(8,128)(2,1)} %basis_in.1, bf16[512,512]{1,0:T(8,128)(2,1)} %basis_out.1, s32[1,256]{1,0:T(1,128)} %membership.1), custom_call_target="tpu_custom_call" | custom-call | tf_op jit(solution)/shard_map/ekfac/pallas_call | solution.py:387
  143.9 2.3 %copy.7 = f32[512,16,32]{0,2,1:T(8,128)} copy(f32[512,16,32]{0,2,1:T(8,128)} %bitcast.3) | data formatting | bytes 2097152

commit v3 on v2

--- a/solution.py
+++ b/solution.py
@@ -212,7 +212,7 @@
         rin["sib"] = send(mine, mine, to_sib)
 
     gat = {}
-    chains = {0: (0, 256, 0), 1: (256, 128, 128)}
+    chains = {0: (0, 192, 64), 1: (256, 128, 128)}
 
     def o_send(key, ref, dev):
         gat[key] = send(ref, ref, dev)
@@ -229,6 +229,13 @@
         rot_out[t, rows] = rotated(1, nh, single, size)
         o_send((nh, "y"), rot_out.at[t, rows], to_yh)
 
+    def o_begin(nh):
+        lo, single, size = chains[nh]
+        rot_out[t, pl.ds(nh * 256, 256)] = rotated(1, nh)
+        o_single(nh, 1)
+        o_send((nh, "y"), rot_out.at[t, pl.ds(lo + single, size)], to_yh)
+        o_cross(nh, 0)
+
     def o_single(nh, s):
         lo, size, _ = chains[nh]
         for d in (1, -1):
@@ -256,9 +263,9 @@
 
     def o_pass(nh, s):
         o_wait(nh, "s", s)
+        o_cross(nh, s)
         if s < 4:
             o_single(nh, s + 1)
-        o_cross(nh, s)
 
     def o_pass_pair(nh, s):
         if s == 0:
@@ -336,9 +343,10 @@
     i_own()
     b_pass(2, 2, True)
     b_pass(2, 2, False)
-    o_start(0)
+    o_begin(0)
     multiply_near(1, n1, -1, 2)
     i_other()
+    o_pass_pair(0, 0)
     b_pass(2, 3, True)
     o_pass(0, 1)
     b_wait(2, 3, False)
@@ -350,14 +358,17 @@
     r_send(1, 1, 128, 128)
     r_send(1, 1, 0, 128)
     o_pass(0, 2)
+    o_pass_pair(0, 1)
     i_sib()
     o_start_pair(1)
     o_start(1)
     o_pass(0, 3)
+    o_pass_pair(0, 2)
     for d in range(1, 16):
         label_copies[d].wait_recv()
     o_pass_pair(1, 0)
     o_pass(0, 4)
+    o_pass_pair(0, 3)
     o_pass(1, 1)
     rin["sib"].wait_recv()
     moments_at(0, 0)
@@ -370,6 +381,7 @@
     o_pass_pair(1, 3)
     o_pass(1, 4)
     moments_at(0, 3)
+    o_wait(0, "p", 4)
     moments_at(0, 4)
     moments_at(1, 0)
     moments_at(1, 1)
@@ -377,7 +389,6 @@
     moments_at(1, 3)
     o_wait(1, "p", 4)
     moments_at(1, 4)
-    out[...] = out[...] * F32(1.0 / 4096)
     for copy in sent:
         copy.wait_send()
 
@@ -406,7 +417,7 @@
             collective_id=0, has_side_effects=True, vmem_limit_bytes=56 * 1024 * 1024),
         name="ekfac",
     )(acts, grads, basis_in, basis_out, membership)
-    return jnp.transpose(energy.reshape(16, 32, 512), (2, 0, 1))
+    return jnp.transpose(energy.reshape(16, 32, 512), (2, 0, 1)) * F32(1.0 / 4096)
 
 
 def solution(mesh):

time: 147 us -> 144 us (0.980)
  Pallas kernels: 144 us -> 141 us
  other arithmetic: 0 us -> 2.29 us
  local copies, waits for them, and re-layouts: 2.29 us -> 0 us
    pallas_call x1, Pallas kernels: 144 us -> 141 us  [local(): pl.pallas_call(kernel, out_shape=jax.ShapeDtypeStruct((512, 512), F32), i...]
    mul x0 -> x1, other arithmetic: none -> 2.29 us  [local(): jnp.transpose(energy.reshape(16, 32, 512), (2, 0, 1)) * F32(1.0 / 4096)]
    unnamed x1 -> x0, local copies, waits for them, and re-layouts: 2.29 us -> none
where the time goes in v3:
time: 144 us; the launch traced here: 143 us
  Pallas kernels  141 us (98%)
  other arithmetic  2.29 us (2%)
    pallas_call x1, Pallas kernels, local(): pl.pallas_call(kernel, out_shape=jax.ShapeDtypeStruct((512, 512), F32), i...  141 us

profile of v3, /device:TPU:10, one launch (start us, length us, event | category | flops | bytes accessed | tf_op | source)
XLA Modules:
  0.0 143.1 jit_solution(11793524585111377363)
XLA Ops:
  0.0 140.8 %ekfac.1 = f32[512,512]{1,0:T(8,128)} custom-call(bf16[256,512]{1,0:T(8,128)(2,1)} %acts.1, bf16[256,512]{1,0:T(8,128)(2,1)} %grads.1, bf16[512,512]{1,0:T(8,128)(2,1)} %basis_in.1, bf16[512,512]{1,0:T(8,128)(2,1)} %basis_out.1, s32[1,256]{1,0:T(1,128)} %membership.1), custom_call_target="tpu_custom_call" | custom-call | tf_op jit(solution)/shard_map/ekfac/pallas_call | solution.py:398
  140.8 2.3 %broadcast_multiply_fusion = f32[512,512]{1,0:T(8,128)} fusion(f32[512,512]{1,0:T(8,128)} %ekfac.1), kind=kLoop, calls=%fused_computation | loop fusion | flops 262144 | bytes 2097152 | tf_op jit(solution)/shard_map/mul | solution.py:420

commit v4 on v3

--- a/solution.py
+++ b/solution.py
@@ -262,6 +262,13 @@
                 gat[nh, kind, s, d].wait_recv()
 
     def o_pass(nh, s):
+        if s == 4:
+            lo, size, _ = chains[nh]
+            for d in (1, -1):
+                gat[nh, "s", 4, d].wait_recv()
+                rows = pl.ds(lo if d == 1 else lo + size // 2, size // 2)
+                o_send((nh, "c", 4, d), rot_out.at[2 * zat(4) + yh, rows], to_yh)
+            return
         o_wait(nh, "s", s)
         o_cross(nh, s)
         if s < 4:

time: 144 us -> 144 us (level)
  no operation moved by 1% of the time
where the time goes in v4:
time: 144 us; the launch traced here: 143 us
  Pallas kernels  141 us (98%)
  other arithmetic  2.29 us (2%)
    pallas_call x1, Pallas kernels, local(): pl.pallas_call(kernel, out_shape=jax.ShapeDtypeStruct((512, 512), F32), i...  141 us

profile of v4, /device:TPU:10, one launch (start us, length us, event | category | flops | bytes accessed | tf_op | source)
XLA Modules:
  0.0 143.1 jit_solution(3620635056236095760)
XLA Ops:
  0.0 140.8 %ekfac.1 = f32[512,512]{1,0:T(8,128)} custom-call(bf16[256,512]{1,0:T(8,128)(2,1)} %acts.1, bf16[256,512]{1,0:T(8,128)(2,1)} %grads.1, bf16[512,512]{1,0:T(8,128)(2,1)} %basis_in.1, bf16[512,512]{1,0:T(8,128)(2,1)} %basis_out.1, s32[1,256]{1,0:T(1,128)} %membership.1), custom_call_target="tpu_custom_call" | custom-call | tf_op jit(solution)/shard_map/ekfac/pallas_call | solution.py:405
  140.8 2.3 %broadcast_multiply_fusion = f32[512,512]{1,0:T(8,128)} fusion(f32[512,512]{1,0:T(8,128)} %ekfac.1), kind=kLoop, calls=%fused_computation | loop fusion | flops 262144 | bytes 2097152 | tf_op jit(solution)/shard_map/mul | solution.py:427
